TPU v7x, 512 devices: a whole 4x8x8 slice. The times are simulated.
512 devices in a mesh: tm: 32 (over x, y), region: 16 (over z, core).
Axes of the slice: x: 4, y: 8, z: 8, core: 2. Of those that a mesh axis runs over, the one named last changes fastest.
Arguments:
- events: float32 [32, 16, 4, 3072], P('tm', 'region'), may hold values from 0 to 32, as said below
- background: float32 [32, 16, 3072], P('tm', 'region'), may hold values from 0.1 to 2
- decays: float32 [16], replicated, may hold values from 0.3 to 30
- widths: float32 [16], replicated, may hold values from 0.05 to 1.5
- mix_start: float32 [16, 16], replicated, may hold values from 0.0005 to 0.006
- rate_start: float32 [1], replicated, may hold values from 0.3 to 3
- pair_block: int32 [32, 16, 6], P('tm', 'region'), may hold values from 0 to 23, as said below
- pair_source: int32 [32, 16, 6], P('tm', 'region'), may hold values from 0 to 287, as said below
- pair_count: int32 [32, 16], P('tm', 'region'), may hold values from 1 to 6, as said below
Outputs:
- mixture: float32 [16, 16], replicated
- base_rate: float32 [1], replicated
- bg_share: float32 [32, 16, 3072], P('tm', 'region')
- offspring: float32 [32, 16, 3072], P('tm', 'region')
Inputs may be any that keep to these rules, and one draw needn't show every extreme that they name: `events`: rows per event: time, in [s, s + 1) on slab s; east position, in [r, r + 1) on region r; north position in [0, 1); magnitude above the threshold in [0, 2]. `pair_block`: a block of the device that holds the slot. `pair_source`: (d * 3 + e) * 24 + b with d < 4; it always names a slab s - d >= 0 and a region r + e - 1 that exist, also in slots that are not live. `pair_count`: some device uses all 6 slots in every draw.
All inputs are finite; a program needn't handle non-finite values.
Results may differ from a plain program's by a relative error of at most 0.0003.
Values sent between devices are 32-bit elements; how exact they have to be, the bound alone decides.
A program may use at most 64 MiB of HBM per device.

v0:
```python
import math

import jax
import jax.numpy as jnp
from jax import lax
from jax.sharding import PartitionSpec as P

NDECAY = 16
NWIDTH = 16
BLK = 128
DEPTH = 4
PMAX = 6
ITERS = 2


PRODUCTIVITY = 1.0


def padded(cells, sides, width):
    for axis, dim in sides:
        count = lax.axis_size(axis)
        ends = count - 1
        head = lax.slice_in_dim(cells, 0, width, axis=dim)
        tail = lax.slice_in_dim(cells, cells.shape[dim] - width, cells.shape[dim], axis=dim)
        cells = jnp.concatenate(
            [
                lax.ppermute(tail, axis, [(i, (i + 1) % count) for i in range(ends)]),
                cells,
                lax.ppermute(head, axis, [((i + 1) % count, i) for i in range(ends)]),
            ],
            axis=dim,
        )
    return cells


def shifted(block, axis, distance):
    devices = range(lax.axis_size(axis))
    route = [(i - distance, i) for i in devices if i - distance in devices]
    return lax.ppermute(block, axis, route)


def pair_tiles(target, source, decays, widths):
    gap_time = target[0][:, None] - source[0][None, :]
    gap_east = target[1][:, None] - source[1][None, :]
    gap_north = target[2][:, None] - source[2][None, :]
    causal = gap_time > 0.0
    elapsed = jnp.where(causal, gap_time, 0.0)
    temporal = jnp.where(
        causal[None], decays[:, None, None] * jnp.exp(-decays[:, None, None] * elapsed[None]), 0.0
    )
    spread = 2.0 * widths * widths
    spatial = (
        jnp.exp(-(gap_east * gap_east + gap_north * gap_north)[None] / spread[:, None, None])
        / (math.pi * spread)[:, None, None]
    )
    return (temporal, spatial)


def excitation(temporal, spatial, mixture, yields):
    weighted = jnp.einsum("kl,lij->kij", mixture, spatial, precision=lax.Precision.HIGHEST)
    return jnp.sum(temporal * weighted, axis=0) * yields[None, :]


def mass_split(temporal, spatial, weights):
    return jnp.einsum(
        "kij,lij->kl", temporal * weights[None], spatial, precision=lax.Precision.HIGHEST
    )


def body(
    events, background, decays, widths, mix_start, rate_start, pair_block, pair_source, pair_count
):
    events_dev = events.shape[3]
    block_count = events_dev // BLK
    own_events = events[0, 0]
    base_level = background[0, 0]
    anchor = jnp.zeros((), jnp.int32)
    nearby = padded(events, (("region", 1),), 1)[0]
    levels = [nearby]
    for time_lag in range(1, DEPTH):
        levels.append(shifted(levels[-1], "tm", 1))
    sources = jnp.stack(levels)
    yield_total = lax.psum(jnp.sum(jnp.exp(PRODUCTIVITY * own_events[3])), ("tm", "region"))
    live_count = pair_count[0, 0]
    target_list = pair_block[0, 0]
    source_list = pair_source[0, 0]
    events_all = events_dev * lax.axis_size("tm") * lax.axis_size("region")

    def fetch_pair(slot_index):
        target_blk = target_list[slot_index]
        candidate = source_list[slot_index]
        time_lag = candidate // (3 * block_count)
        region_side = candidate // block_count % 3
        source_blk = candidate % block_count
        target = lax.dynamic_slice(own_events, (anchor, target_blk * BLK), (4, BLK))
        source = lax.dynamic_slice(
            sources, (time_lag, region_side, anchor, source_blk * BLK), (1, 1, 4, BLK)
        )[0, 0]
        temporal, spatial = pair_tiles(target, source, decays, widths)
        return (
            target_blk,
            time_lag,
            region_side,
            source_blk,
            temporal,
            spatial,
            jnp.exp(PRODUCTIVITY * source[3]),
        )

    def run_slots(slot_step, initial):

        def masked(slot_index, carry):
            return slot_step(slot_index, carry, (slot_index < live_count).astype(jnp.float32))

        result = lax.fori_loop(0, PMAX, masked, initial)
        return result

    mixture = mix_start
    base_rate = rate_start[0]
    bg_share = base_level
    spent = jnp.zeros((DEPTH, 3, events_dev), jnp.float32)
    for sweep in range(ITERS):

        def add_trigger(slot_index, running, live_flag):
            target_blk, time_lag, region_side, source_blk, temporal, spatial, yields = fetch_pair(
                slot_index
            )
            row_sums = jnp.sum(excitation(temporal, spatial, mixture, yields), axis=1) * live_flag
            offset = target_blk * BLK
            return lax.dynamic_update_slice(
                running, lax.dynamic_slice(running, (offset,), (BLK,)) + row_sums, (offset,)
            )

        triggered = run_slots(add_trigger, jnp.zeros((events_dev,), jnp.float32))
        intensity = base_rate * base_level + triggered
        inverse = 1.0 / intensity

        def split_pair(slot_index, carry, live_flag):
            scores, spent_now = carry
            target_blk, time_lag, region_side, source_blk, temporal, spatial, yields = fetch_pair(
                slot_index
            )
            weights = lax.dynamic_slice(inverse, (target_blk * BLK,), (BLK,)) * live_flag
            trigger = excitation(temporal, spatial, mixture, yields) * weights[:, None]
            place_at = (time_lag, region_side, source_blk * BLK)
            before = lax.dynamic_slice(spent_now, place_at, (1, 1, BLK))
            spent_now = lax.dynamic_update_slice(
                spent_now, before + jnp.sum(trigger, axis=0)[None, None], place_at
            )
            scores = scores + mass_split(temporal, spatial, weights[:, None] * yields[None, :])
            return (scores, spent_now)

        initial = (
            jnp.zeros((NDECAY, NWIDTH), jnp.float32),
            jnp.zeros((DEPTH, 3, events_dev), jnp.float32),
        )
        scores, spent = run_slots(split_pair, initial)
        bg_share = base_rate * base_level * inverse
        totals = lax.psum((scores, jnp.sum(bg_share)), ("tm", "region"))
        mixture = mixture * totals[0] / yield_total
        base_rate = totals[1] / events_all
    returned = spent[DEPTH - 1]
    for time_lag in range(DEPTH - 2, -1, -1):
        returned = spent[time_lag] + shifted(returned, "tm", -1)
    offspring = returned[1] + shifted(returned[0], "region", -1)
    offspring = offspring + shifted(returned[2], "region", 1)
    return (mixture, jnp.reshape(base_rate, (1,)), bg_share[None, None], offspring[None, None])


def solution(mesh):
    placed = (
        P("tm", "region", None, None),
        P("tm", "region", None),
        P(),
        P(),
        P(),
        P(),
        P("tm", "region", None),
        P("tm", "region", None),
        P("tm", "region"),
    )
    return jax.shard_map(
        body,
        mesh=mesh,
        in_specs=placed,
        out_specs=(P(), P(), P("tm", "region", None), P("tm", "region", None)),
        check_vma=False,
    )
```

profile of v0, /device:TPU:1, one launch (start us, length us, event | category | flops | bytes accessed | tf_op | source)
XLA Modules:
  0.0 470.9 jit_solution(9898130457534486490)
XLA Ops:
  0.6 5.5 %collective-permute-start = (f32[1,1,4,3072]{3,2,1,0:T(4,128)}, f32[1,1,4,3072]{3,2,1,0:T(4,128)S(1)}, u32[]{:S(2)}, u32[]{:S(2)}) collective-permute-start(f32[1,1,4,3072]{3,2,1,0:T(4,128)} %param.17), channel_id=1, source_target_pairs={{0,1},{1,2},{2,3},{3,4},{4,5},{5,6},{6,7},{7,8},{8,9},{9,10},{10,1... | collective-permute-start | bytes 147464 | tf_op jit(solution)/shard_map/ppermute | solution.py:27
  6.2 4.7 collective-permute-start.1
  11.9 3.1 collective-permute-start.2
  15.7 1.8 collective-permute-done.2
  17.4 3.8 collective-permute-start.3
  21.3 3.5 collective-permute-done.3
  24.8 3.9 collective-permute-start.4
  29.4 2.1 collective-permute-done.4
  32.4 47.5 %while.68 = (s32[]{:T(128)}, f32[3072]{0:T(1024)S(1)}, s32[6]{0:T(128)S(1)}, f32[4,3072]{1,0:T(4,128)S(1)}, s32[6]{0:T(128)S(1)}, /*index=5*/f32[4,3,4,3072]{3,2...) while((s32[]{:T(128)}, f32[3072]{0:T(1024)S(1)}, ...), condition=%wide.region_3.4_spmd, body=%wide.region_0.3_spmd.sunk | while | flops 52363480 | bytes 450149 | solution.py:115
  45.7 1.5 fusion.70
  53.7 1.5 fusion.70
  80.5 49.0 %while.70 = (s32[]{:T(128)}, f32[16,16]{1,0:T(8,128)S(1)}, s32[6]{0:T(128)S(1)}, f32[4,3072]{1,0:T(4,128)S(1)}, s32[6]{0:T(128)S(1)}, /*index=5*/f32[4,3,4,3072]...) while((s32[]{:T(128)}, f32[16,16]{1,0:T(8,128)S(1)}, ...), condition=%wide.region_5.6_spmd.clone, body=%wide.region_4.5_spmd.clone.sunk | while | flops 52101848 | bytes 450671 | solution.py:115
  86.7 1.9 fusion.76
  94.9 1.9 fusion.76
  103.1 1.9 fusion.76
  111.2 1.9 fusion.76
  119.4 1.9 fusion.76
  127.6 1.9 fusion.76
  129.5 108.4 %all-reduce.1 = (f32[16,16]{1,0:T(8,128)S(1)}, f32[]{:T(128)}, f32[]{:T(128)}) all-reduce(f32[16,16]{1,0:T(8,128)S(1)} %get-tuple-element.1230, f32[]{:T(128)} %exponential_reduce_fusion, f32[]{:T(128)} %get-tuple-element.1461), channel_id=1, replica_groups=mesh['tm'=32,'region'=16] {'tm','region'}, use_global_device_ids=true, to_apply=%region_6.7 | all-reduce | flops 258 | bytes 2064 | tf_op jit(solution)/shard_map/psum | solution.py:159
  239.3 47.6 %while.69 = (s32[]{:T(128)}, f32[3072]{0:T(1024)S(1)}, s32[6]{0:T(128)S(1)}, f32[4,3072]{1,0:T(4,128)S(1)}, s32[6]{0:T(128)S(1)}, /*index=5*/f32[4,3,4,3072]{3,2...) while((s32[]{:T(128)}, f32[3072]{0:T(1024)S(1)}, ...), condition=%wide.region_14.15_spmd, body=%wide.region_11.14_spmd.sunk | while | flops 52363480 | bytes 450149 | solution.py:115
  288.1 59.5 %while.71 = (s32[]{:T(128)}, f32[16,16]{1,0:T(8,128)S(1)}, f32[4,3,3072]{2,1,0:T(4,128)S(1)}, s32[6]{0:T(128)S(1)}, f32[4,3072]{1,0:T(4,128)S(1)}, /*index=5*/s3...) while((s32[]{:T(128)}, f32[16,16]{1,0:T(8,128)S(1)}, ...), condition=%wide.region_18.19_spmd.clone, body=%wide.region_15.18_spmd.clone.sunk | while | flops 104301272 | bytes 733583 | solution.py:115
  295.9 1.9 fusion.82
  305.8 1.9 fusion.82
  315.8 1.9 fusion.82
  325.7 1.9 fusion.82
  335.6 1.9 fusion.82
  345.5 1.9 fusion.82
  349.0 3.5 collective-permute-done.5
  353.8 3.5 collective-permute-done.6
  358.7 101.6 %all-reduce = (f32[16,16]{1,0:T(8,128)S(1)}, f32[]{:T(128)}) all-reduce(f32[16,16]{1,0:T(8,128)S(1)} %get-tuple-element.1232, f32[]{:T(128)} %get-tuple-element.1409), channel_id=1, replica_groups=mesh['tm'=32,'region'=16] {'tm','region'}, use_global_device_ids=true, to_apply=%region_19.20 | all-reduce | flops 257 | bytes 2056 | tf_op jit(solution)/shard_map/psum | solution.py:159
  460.4 3.8 collective-permute-start.9
  464.2 1.9 collective-permute-start.8
  (337 shorter events, 79.3 us)
Async XLA Ops:
  0.6 10.3 %copy-start = (f32[1,1,4,3072]{3,2,1,0:T(4,128)S(1)}, f32[1,1,4,3072]{3,2,1,0:T(4,128)}, u32[]{:S(2)}) copy-start(f32[1,1,4,3072]{3,2,1,0:T(4,128)} %param.17) | copy-start | bytes 147460
  0.6 10.2 %collective-permute-start = (f32[1,1,4,3072]{3,2,1,0:T(4,128)}, f32[1,1,4,3072]{3,2,1,0:T(4,128)S(1)}, u32[]{:S(2)}, u32[]{:S(2)}) collective-permute-start(f32[1,1,4,3072]{3,2,1,0:T(4,128)} %param.17), channel_id=1, source_target_pairs={{0,1},{1,2},{2,3},{3,4},{4,5},{5,6},{6,7},{7,8},{8,9},{9,10},{10,1... | collective-permute-start | bytes 147464 | tf_op jit(solution)/shard_map/ppermute | solution.py:27
  6.2 5.8 %collective-permute-start.1 = (f32[1,1,4,3072]{3,2,1,0:T(4,128)}, f32[1,1,4,3072]{3,2,1,0:T(4,128)S(1)}, u32[]{:S(2)}, u32[]{:S(2)}) collective-permute-start(f32[1,1,4,3072]{3,2,1,0:T(4,128)} %param.17), channel_id=1, source_target_pairs={{1,0},{2,1},{3,2},{4,3},{5,4},{6,5},{7,6},{8,7},{9,8},{10,9},{11,1... | collective-permute-start | bytes 147464 | tf_op jit(solution)/shard_map/ppermute | solution.py:29
  11.9 9.3 %copy-start.1 = (f32[1,1,3072]{2,1,0:T(1,128)S(1)}, f32[1,1,3072]{2,1,0:T(1,128)}, u32[]{:S(2)}) copy-start(f32[1,1,3072]{2,1,0:T(1,128)} %param.18) | copy-start | bytes 36868
  11.9 5.5 %collective-permute-start.2 = (f32[3,4,3072]{2,1,0:T(4,128)S(1)}, f32[3,4,3072]{2,1,0:T(4,128)S(1)}, u32[]{:S(2)}, u32[]{:S(2)}) collective-permute-start(f32[3,4,3072]{2,1,0:T(4,128)S(1)} %bitcast.239), channel_id=1, source_target_pairs={{0,16},{16,32},{32,48},{48,64},{64,80},{80,96},{96,112},{112,128},... | collective-permute-start | bytes 442376 | tf_op jit(solution)/shard_map/ppermute | solution.py:39
  17.4 7.4 %collective-permute-start.3 = (f32[3,4,3072]{2,1,0:T(4,128)S(1)}, f32[3,4,3072]{2,1,0:T(4,128)S(1)}, u32[]{:S(2)}, u32[]{:S(2)}) collective-permute-start(f32[3,4,3072]{2,1,0:T(4,128)S(1)} %collective-permute-done.2), channel_id=1, source_target_pairs={{0,16},{16,32},{32,48},{48,64},{64,80},{80,96},{96,112},{112,128},... | collective-permute-start | bytes 442376 | tf_op jit(solution)/shard_map/ppermute | solution.py:39
  21.3 7.5 %copy-start.5 = (f32[16]{0:T(128)S(1)}, f32[16]{0:T(128)}, u32[]{:S(2)}) copy-start(f32[16]{0:T(128)} %param.19) | copy-start | bytes 196
  24.8 6.7 %collective-permute-start.4 = (f32[3,4,3072]{2,1,0:T(4,128)S(1)}, f32[3,4,3072]{2,1,0:T(4,128)S(1)}, u32[]{:S(2)}, u32[]{:S(2)}) collective-permute-start(f32[3,4,3072]{2,1,0:T(4,128)S(1)} %collective-permute-done.3), channel_id=1, source_target_pairs={{0,16},{16,32},{32,48},{48,64},{64,80},{80,96},{96,112},{112,128},... | collective-permute-start | bytes 442376 | tf_op jit(solution)/shard_map/ppermute | solution.py:39
  31.7 0.7 copy-start.2
  31.7 0.7 copy-start.3
  31.7 0.7 copy-start.4
  31.7 0.7 copy-start.6
  347.7 4.8 %collective-permute-start.5 = (f32[3,3072]{1,0:T(4,128)S(1)}, f32[3,3072]{1,0:T(4,128)S(1)}, u32[]{:S(2)}, u32[]{:S(2)}) collective-permute-start(f32[3,3072]{1,0:T(4,128)S(1)} %slice_bitcast_fusion.24), channel_id=1, source_target_pairs={{16,0},{32,16},{48,32},{64,48},{80,64},{96,80},{112,96},{128,112},... | collective-permute-start | bytes 110600 | tf_op jit(solution)/shard_map/ppermute | solution.py:39
  352.5 4.8 %collective-permute-start.6 = (f32[3,3072]{1,0:T(4,128)S(1)}, f32[3,3072]{1,0:T(4,128)S(1)}, u32[]{:S(2)}, u32[]{:S(2)}) collective-permute-start(f32[3,3072]{1,0:T(4,128)S(1)} %bitcast_add_fusion.1), channel_id=1, source_target_pairs={{16,0},{32,16},{48,32},{64,48},{80,64},{96,80},{112,96},{128,112},... | collective-permute-start | bytes 110600 | tf_op jit(solution)/shard_map/ppermute | solution.py:39
  357.4 102.9 %collective-permute-start.7 = (f32[3,3072]{1,0:T(4,128)S(1)}, f32[3,3072]{1,0:T(4,128)S(1)}, u32[]{:S(2)}, u32[]{:S(2)}) collective-permute-start(f32[3,3072]{1,0:T(4,128)S(1)} %bitcast_add_fusion.2), channel_id=1, source_target_pairs={{16,0},{32,16},{48,32},{64,48},{80,64},{96,80},{112,96},{128,112},... | collective-permute-start | bytes 110600 | tf_op jit(solution)/shard_map/ppermute | solution.py:39
  460.4 7.7 %collective-permute-start.9 = (f32[3072]{0:T(1024)S(1)}, f32[3072]{0:T(1024)S(1)}, u32[]{:S(2)}, u32[]{:S(2)}) collective-permute-start(f32[3072]{0:T(1024)S(1)} %bitcast.248), channel_id=1, source_target_pairs={{0,1},{1,2},{2,3},{3,4},{4,5},{5,6},{6,7},{7,8},{8,9},{9,10},{10,1... | collective-permute-start | bytes 36872 | tf_op jit(solution)/shard_map/ppermute | solution.py:39
  464.2 5.0 %collective-permute-start.8 = (f32[3072]{0:T(1024)S(1)}, f32[3072]{0:T(1024)S(1)}, u32[]{:S(2)}, u32[]{:S(2)}) collective-permute-start(f32[3072]{0:T(1024)S(1)} %bitcast.247), channel_id=1, source_target_pairs={{1,0},{2,1},{3,2},{4,3},{5,4},{6,5},{7,6},{8,7},{9,8},{10,9},{11,1... | collective-permute-start | bytes 36872 | tf_op jit(solution)/shard_map/ppermute | solution.py:39
where the time goes:
time: 473 us; the launch traced here: 471 us
  blocking collectives  210 us (44%)
  loops' own time  110 us (23%)
  matrix products  50.5 us (11%)
  local copies, waits for them, and re-layouts  32.3 us (7%)
  starting transfers between devices  30.6 us (6%)
  waiting for transfers between devices  16.7 us (4%)
  other arithmetic  16.4 us (3%)
    psum x2, blocking collectives, body(): totals = lax.psum((scores, jnp.sum(bg_share)), ('tm', 'region'))  210 us
    another operation x4, loops' own time, run_slots(): result = lax.fori_loop(0, PMAX, masked, initial)  110 us
    dot_general x18, matrix products, excitation(): jnp.einsum('kl,lij->kij', mixture, spatial, precision=lax.Precision.HIGHEST)  27.6 us
    dot_general x12, matrix products, mass_split(): jnp.einsum('kij,lij->kl', temporal * weights[None], spatial, precision=la...  23 us
    ppermute x8, starting transfers between devices, shifted(): return lax.ppermute(block, axis, route)  20.4 us
    ppermute x8, waiting for transfers between devices, shifted(): return lax.ppermute(block, axis, route)  15.6 us
    dynamic_slice x24, local copies, waits for them, and re-layouts, fetch_pair(): candidate = source_list[slot_index]  15 us
    dynamic_slice x24, local copies, waits for them, and re-layouts, fetch_pair(): target_blk = target_list[slot_index]  15 us
  transfers between devices with their start and end apart: 10, of which 7 were waited for; matrix products, arithmetic and copies ran while one was open for 0% of the time, Pallas kernels for 0%

commit v1 on v0

v1 whole, which is shorter than its diff:
```python
import math

import jax
import jax.numpy as jnp
from jax import lax
from jax.experimental import pallas as pl
from jax.experimental.pallas import tpu as pltpu
from jax.sharding import PartitionSpec as P

NK = 16
NL = 16
BLK = 128
NBLK = 24
DEPTH = 4
PMAX = 6
ITERS = 2
CELL = 3 * NBLK
NEAR = 3 * DEPTH - 1
FAR = 1.0e6
MESH = pl.DeviceIdType.MESH
PRODUCTIVITY = 1.0


def split_bf16(value):
    high = value.astype(jnp.bfloat16)
    low = (value - high.astype(jnp.float32)).astype(jnp.bfloat16)
    return high, low


def stacked_rows(value):
    high, low = split_bf16(value)
    return jnp.concatenate(
        [
            jnp.concatenate([high, high], axis=1),
            jnp.concatenate([low, jnp.zeros_like(low)], axis=1),
        ],
        axis=0,
    )


def columns(rows):
    return jnp.transpose(jnp.concatenate([rows, rows], axis=0))


def kernel(
    n_tm,
    n_region,
    ev_in,
    bg_in,
    decays_in,
    widths_in,
    mix_in,
    rate_s,
    block_in,
    source_in,
    count_s,
    mix_out,
    rate_out,
    share_out,
    offspring_out,
    bg_ref,
    decays_s,
    widths_s,
    mix_ref,
    block_s,
    source_s,
    events,
    request,
    requests,
    requests_s,
    answer,
    picked,
    falloff,
    stats,
    early,
    late,
    coeff,
    payload,
    partial,
    returned,
    local_sem,
    request_send,
    request_recv,
    event_send,
    event_recv,
    answer_send,
    answer_recv,
    return_send,
    return_recv,
    sum_send,
    sum_recv,
):
    slab = lax.axis_index("tm")
    zone = lax.axis_index("region")
    events_all = float(n_tm * n_region * NBLK * BLK)
    lengths = (n_region, n_tm)
    my_place = (zone, slab)

    def wrapped(place, step, length):
        moved = place + step
        return jnp.where(moved >= length, moved - length, jnp.where(moved < 0, moved + length, moved))

    def device(lag, side):
        return (wrapped(slab, lag, n_tm), wrapped(zone, side, n_region))

    def peer(axis, step):
        if axis == 0:
            return (slab, wrapped(zone, step, n_region))
        return (wrapped(slab, step, n_tm), zone)

    staged = (
        (source_in, source_s),
        (block_in, block_s),
        (decays_in, decays_s),
        (widths_in, widths_s),
        (mix_in, mix_ref),
        (bg_in, bg_ref),
        (ev_in, events.at[pl.ds(NBLK, NBLK)]),
    )
    staging = [
        pltpu.make_async_copy(src, dst, local_sem.at[index])
        for index, (src, dst) in enumerate(staged)
    ]
    for copy in staging:
        copy.start()

    barrier = pltpu.get_barrier_semaphore()
    near = [(lag, 0) for lag in range(1, DEPTH)]
    near += [(lag, side) for lag in range(DEPTH) for side in (-1, 1)]
    greeted = [(-lag, side) for lag, side in near] + [(lag, -side) for lag, side in near if lag]
    greeted += [(0, step) for step in range(2, n_region - 1)]
    greeted += [(step, 0) for step in range(DEPTH, n_tm - DEPTH + 1)]
    for place in greeted:
        pl.semaphore_signal(barrier, inc=1, device_id=device(*place), device_id_type=MESH)
    staging[0].wait()
    lane = lax.broadcasted_iota(jnp.int32, (1, BLK), 1)
    asked = jnp.zeros((1, BLK), jnp.int32)
    for p in range(PMAX):
        asked = jnp.where(lane == p, source_s[0, 0, p], asked)
    request[...] = asked
    pl.semaphore_wait(barrier, len(greeted))

    pending = []

    def send(src, dst, send_sem, recv_sem, device):
        copy = pltpu.make_async_remote_copy(
            src_ref=src,
            dst_ref=dst,
            send_sem=send_sem,
            recv_sem=recv_sem,
            device_id=device,
            device_id_type=MESH,
        )
        copy.start()
        pending.append(copy)
        return copy

    event_copies = [
        send(
            ev_in,
            events.at[pl.ds(2 * NBLK * side, NBLK)],
            event_send.at[side],
            event_recv.at[side],
            device(0, 1 - 2 * side),
        )
        for side in range(2)
    ]
    request_copies = [
        send(
            request,
            requests.at[index],
            request_send.at[index],
            request_recv.at[index],
            device(-lag, side),
        )
        for index, (lag, side) in enumerate(near)
    ]

    for copy in staging[1:]:
        copy.wait()
    decay_col = jnp.zeros((NK, BLK), jnp.float32)
    row16 = lax.broadcasted_iota(jnp.int32, (NK, BLK), 0)
    for k in range(NK):
        decay_col = jnp.where(row16 == k, decays_s[k], decay_col)
    width_col = jnp.zeros((NL, BLK), jnp.float32)
    for l in range(NL):
        width_col = jnp.where(row16 == l, widths_s[l], width_col)
    spread = 2.0 * width_col * width_col
    coeff[0] = -math.log2(math.e) / spread
    coeff[1] = 1.0 / (math.pi * spread)
    mix_tile = mix_ref[...]
    mixture = [jnp.broadcast_to(mix_tile[:, l : l + 1], (NK, BLK)) for l in range(NL)]
    mixture = jnp.concatenate(mixture, axis=0)
    own_yield = jnp.sum(jnp.exp(PRODUCTIVITY * events[pl.ds(NBLK, NBLK), 3, :]), axis=0, keepdims=True)
    own_yield = jnp.broadcast_to(jnp.sum(own_yield, axis=1, keepdims=True), (1, BLK))

    askers = DEPTH - 1
    for copy in request_copies[:askers]:
        copy.wait_recv()
    scalar_copies = [
        pltpu.make_async_copy(requests.at[part], requests_s.at[part], local_sem.at[len(staged) + half])
        for half, part in enumerate((pl.ds(0, askers), pl.ds(askers, len(near) - askers)))
    ]
    scalar_copies[0].start()
    scalar_copies[0].wait()
    for copy in event_copies:
        copy.wait_recv()

    def cell_of(relative):
        inside = jnp.logical_and(relative >= 0, relative < CELL)
        return jnp.where(inside, relative, 0)

    answer_copies = []
    for lag in range(DEPTH - 1, 0, -1):
        for p in range(PMAX):
            answer[lag - 1, p] = events[cell_of(requests_s[lag - 1, 0, p] - lag * CELL)]
        answer_copies.append(
            send(
                answer.at[lag - 1],
                picked.at[lag],
                answer_send.at[lag - 1],
                answer_recv.at[lag - 1],
                device(lag, 0),
            )
        )
    for p in range(PMAX):
        picked[0, p] = events[cell_of(source_s[0, 0, p])]
    for copy in answer_copies:
        copy.wait_recv()

    start_time = slab.astype(jnp.float32)
    live_count = count_s[0, 0]

    def members(p):
        candidate = source_s[0, 0, p]
        lag = (
            (candidate >= CELL).astype(jnp.int32)
            + (candidate >= 2 * CELL).astype(jnp.int32)
            + (candidate >= 3 * CELL).astype(jnp.int32)
        )
        return picked[lag, p], events[NBLK + block_s[0, 0, p]]

    def distances(target, source):
        gap_time = target[0] - source[0]
        gap_east = target[1] - source[1]
        gap_north = target[2] - source[2]
        square = gap_east * gap_east + gap_north * gap_north
        return jnp.where(gap_time > 0.0, square, FAR)

    def fall(square, l):
        return split_bf16(jnp.exp2(square * coeff[0, l : l + 1, :]))

    def prepare(p, carry):
        source, target = members(p)
        live = jnp.where(p < live_count, 1.0, 0.0)
        after = decay_col * jnp.exp(-decay_col * (target[0:1] - start_time)) * live
        before = jnp.exp(decay_col * (source[0:1] - start_time)) * jnp.exp(PRODUCTIVITY * source[3:4])
        late[p] = after
        early[p] = before
        left = stacked_rows(before)
        cols = columns(source)
        square = distances(
            [target[c : c + 1] for c in range(3)], [cols[:, c : c + 1] for c in range(3)]
        )
        for pair in range(NL // 2):
            parts = [
                jnp.concatenate(fall(square, l), axis=0) for l in (2 * pair, 2 * pair + 1)
            ]
            right = jnp.concatenate(parts, axis=1)
            both = jnp.dot(left, right, preferred_element_type=jnp.float32)
            both = both[:NK] + both[NK:]
            for side in range(2):
                l = 2 * pair + side
                stats[p, l * NK : (l + 1) * NK, :] = (
                    both[:, side * BLK : (side + 1) * BLK] * after * coeff[1, l : l + 1, :]
                )
        return carry

    lax.fori_loop(0, PMAX, prepare, 0)

    def prepare_back(p, carry):
        source, target = members(p)
        cols = columns(target)
        square = distances(
            [cols[:, c : c + 1] for c in range(3)], [source[c : c + 1] for c in range(3)]
        )
        for l in range(NL):
            falloff[p, l, 0], falloff[p, l, 1] = fall(square, l)
        return carry

    block_row = lax.broadcasted_iota(jnp.int32, (NBLK, BLK), 0)
    background = bg_ref[...]

    def expect(mixture, rate):
        triggered = jnp.zeros((NBLK, BLK), jnp.float32)
        for p in range(PMAX):
            row = jnp.sum(stats[p] * mixture, axis=0, keepdims=True)
            triggered = triggered + jnp.where(block_row == block_s[0, 0, p], row, 0.0)
        level = rate * background
        inverse = 1.0 / (level + triggered)
        share = level * inverse
        weights = [
            jnp.sum(jnp.where(block_row == block_s[0, 0, p], inverse, 0.0), axis=0, keepdims=True)
            for p in range(PMAX)
        ]
        scores = stats[0] * weights[0]
        for p in range(1, PMAX):
            scores = scores + stats[p] * weights[p]
        rows = [
            jnp.sum(jnp.transpose(scores[half * BLK : (half + 1) * BLK]), axis=0, keepdims=True)
            for half in range(2)
        ]
        total = jnp.sum(jnp.sum(share, axis=0, keepdims=True), axis=1, keepdims=True)
        rows.append(jnp.broadcast_to(total, (1, BLK)))
        rows.append(own_yield)
        return share, weights, jnp.concatenate(rows, axis=0)

    def start_sum(stage, axis, value):
        payload[stage] = value
        partial[stage, my_place[axis]] = value
        for step in range(1, lengths[axis]):
            pltpu.make_async_remote_copy(
                src_ref=payload.at[stage],
                dst_ref=partial.at[stage, my_place[axis]],
                send_sem=sum_send.at[stage],
                recv_sem=sum_recv.at[stage],
                device_id=peer(axis, step),
                device_id_type=MESH,
            ).start()

    def others(stage, axis, sems):
        part = partial.at[stage, pl.ds(0, lengths[axis] - 1)]
        return pltpu.make_async_copy(part, part, sems.at[stage])

    def end_sum(stage, axis):
        others(stage, axis, sum_recv).wait()
        return jnp.sum(partial[stage, 0 : lengths[axis]], axis=0)

    def update(mixture, total):
        cols = columns(total)
        factor = jnp.concatenate(
            [jnp.broadcast_to(cols[:, half : half + 1], (BLK, BLK)) for half in range(2)], axis=0
        )
        return mixture * factor / total[3:4, :], total[2:3, :] / events_all

    share, weights, value = expect(mixture, jnp.full((1, BLK), rate_s[0], jnp.float32))
    for axis in range(2):
        start_sum(axis, axis, value)
        lax.fori_loop(axis * PMAX // 2, (axis + 1) * PMAX // 2, prepare_back, 0)
        if axis == 0:
            for copy in request_copies[askers:]:
                copy.wait_recv()
            scalar_copies[1].start()
        else:
            scalar_copies[1].wait()
            for copy in pending:
                copy.wait_send()
            pending.clear()
        value = end_sum(axis, axis)
    mixture, rate = update(mixture, value)

    share, weights, value = expect(mixture, rate)
    start_sum(2, 0, value)
    share_out[...] = share
    scaled = mixture * jnp.concatenate(
        [jnp.broadcast_to(coeff[1, l : l + 1, :], (NK, BLK)) for l in range(NL)], axis=0
    )

    for p in range(PMAX):
        late[p] = late[p] * weights[p]

    stats[0] = scaled

    def give_back(p, rows):
        left = stacked_rows(late[p])
        gathered = jnp.zeros((NK, BLK), jnp.float32)
        for pair in range(NL // 2):
            right = jnp.concatenate(
                [
                    jnp.concatenate([falloff[p, l, 0], falloff[p, l, 1]], axis=0)
                    for l in (2 * pair, 2 * pair + 1)
                ],
                axis=1,
            )
            both = jnp.dot(left, right, preferred_element_type=jnp.float32)
            both = both[:NK] + both[NK:]
            for side in range(2):
                l = 2 * pair + side
                gathered = gathered + both[:, side * BLK : (side + 1) * BLK] * stats[0, l * NK : (l + 1) * NK, :]
        row = jnp.sum(gathered * early[p], axis=0, keepdims=True)
        return jnp.where(lax.broadcasted_iota(jnp.int32, (8, BLK), 0) == p, row, rows)

    rows = lax.fori_loop(0, PMAX, give_back, jnp.zeros((8, BLK), jnp.float32))
    returned[0] = rows
    return_copies = [
        send(
            returned.at[0],
            returned.at[index + 1],
            return_send.at[index],
            return_recv.at[index],
            device(-lag, side),
        )
        for index, (lag, side) in enumerate(near)
    ]
    value = end_sum(2, 0)
    start_sum(3, 1, value)

    for copy in return_copies:
        copy.wait_recv()
    gathered = jnp.zeros((NBLK, BLK), jnp.float32)
    for index, (lag, side) in enumerate([(0, 0)] + near):
        first = (lag * 3 + side + 1) * NBLK
        for p in range(PMAX):
            named = source_s[0, 0, p] if index == 0 else requests_s[index - 1, 0, p]
            gathered = gathered + jnp.where(
                block_row == named - first, returned[index, p : p + 1, :], 0.0
            )
    offspring_out[...] = gathered
    for copy in pending:
        copy.wait_send()
    for stage in range(3):
        others(stage, stage % 2, sum_send).wait()
    value = end_sum(3, 1)
    others(3, 1, sum_send).wait()
    mixture, rate = update(mixture, value)
    lane16 = lax.broadcasted_iota(jnp.int32, (NK, BLK), 1)
    square_mix = jnp.zeros((NK, BLK), jnp.float32)
    for l in range(NL):
        square_mix = jnp.where(lane16 == l, mixture[l * NK : (l + 1) * NK], square_mix)
    mix_out[...] = square_mix[:, :NL]
    rate_out[...] = rate[:, 0:1]


def finish(*refs):
    arrived, handed, sems = refs[:4], refs[4:8], refs[8]
    copies = [
        pltpu.make_async_copy(src, dst, sems.at[index])
        for index, (src, dst) in enumerate(zip(arrived, handed))
    ]
    for copy in copies:
        copy.start()
    for copy in copies:
        copy.wait()


def solution(mesh):
    n_tm, n_region = mesh.shape["tm"], mesh.shape["region"]

    def body(
        events, background, decays, widths, mix_start, rate_start, pair_block, pair_source, pair_count
    ):
        blocks = jnp.transpose(jnp.reshape(events, (4, NBLK, BLK)), (1, 0, 2))
        smem = pl.BlockSpec(memory_space=pltpu.SMEM)
        hbm = pl.BlockSpec(memory_space=pltpu.HBM)
        vmem = pl.BlockSpec(memory_space=pltpu.VMEM)
        f32 = jnp.float32
        dma = pltpu.SemaphoreType.DMA
        results = [
            jax.ShapeDtypeStruct((NK, NL), f32),
            jax.ShapeDtypeStruct((1, 1), f32),
            jax.ShapeDtypeStruct((NBLK, BLK), f32),
            jax.ShapeDtypeStruct((NBLK, BLK), f32),
        ]
        found = pl.pallas_call(
            lambda *refs: kernel(n_tm, n_region, *refs),
            out_shape=[pltpu.VMEM(leaf.shape, leaf.dtype) for leaf in results],
            in_specs=[hbm] * 5 + [smem, hbm, hbm, smem],
            out_specs=[vmem] * 4,
            scratch_shapes=[
                pltpu.VMEM((NBLK, BLK), f32),
                pltpu.SMEM(decays.shape, f32),
                pltpu.SMEM(widths.shape, f32),
                pltpu.VMEM(mix_start.shape, f32),
                pltpu.SMEM(pair_block.shape, jnp.int32),
                pltpu.SMEM(pair_source.shape, jnp.int32),
                pltpu.VMEM((CELL, 4, BLK), f32),
                pltpu.VMEM((1, BLK), jnp.int32),
                pltpu.VMEM((NEAR, 1, BLK), jnp.int32),
                pltpu.SMEM((NEAR, 1, BLK), jnp.int32),
                pltpu.VMEM((DEPTH - 1, PMAX, 4, BLK), f32),
                pltpu.VMEM((DEPTH, PMAX, 4, BLK), f32),
                pltpu.VMEM((PMAX, NL, 2, BLK, BLK), jnp.bfloat16),
                pltpu.VMEM((PMAX, NK * NL, BLK), f32),
                pltpu.VMEM((PMAX, NK, BLK), f32),
                pltpu.VMEM((PMAX, NK, BLK), f32),
                pltpu.VMEM((2, NL, BLK), f32),
                pltpu.VMEM((2 * ITERS, 4, BLK), f32),
                pltpu.VMEM((2 * ITERS, max(n_tm, n_region), 4, BLK), f32),
                pltpu.VMEM((NEAR + 1, 8, BLK), f32),
                dma((9,)),
                dma((NEAR,)),
                dma((NEAR,)),
                dma((2,)),
                dma((2,)),
                dma((DEPTH - 1,)),
                dma((DEPTH - 1,)),
                dma((NEAR,)),
                dma((NEAR,)),
                dma((2 * ITERS,)),
                dma((2 * ITERS,)),
            ],
            compiler_params=pltpu.CompilerParams(
                collective_id=0, has_side_effects=True, vmem_limit_bytes=60 * 2**20
            ),
            name="etas_em",
        )(
            blocks,
            jnp.reshape(background, (NBLK, BLK)),
            decays,
            widths,
            mix_start,
            rate_start,
            pair_block,
            pair_source,
            pair_count,
        )
        mixture, rate, share, offspring = pl.pallas_call(
            finish,
            out_shape=results,
            in_specs=[vmem] * 4,
            out_specs=[hbm] * 4,
            scratch_shapes=[dma((4,))],
            compiler_params=pltpu.CompilerParams(vmem_limit_bytes=2**20),
            name="hand_on",
        )(*found)
        return (
            mixture,
            jnp.reshape(rate, (1,)),
            jnp.reshape(share, (1, 1, NBLK * BLK)),
            jnp.reshape(offspring, (1, 1, NBLK * BLK)),
        )

    placed = (
        P("tm", "region", None, None),
        P("tm", "region", None),
        P(),
        P(),
        P(),
        P(),
        P("tm", "region", None),
        P("tm", "region", None),
        P("tm", "region"),
    )
    return jax.shard_map(
        body,
        mesh=mesh,
        in_specs=placed,
        out_specs=(P(), P(), P("tm", "region", None), P("tm", "region", None)),
        check_vma=False,
    )
```

time: 473 us -> 57 us (0.12)
  blocking collectives: 210 us -> 0 us
  loops' own time: 110 us -> 0 us
  Pallas kernels: 0 us -> 54.9 us
  matrix products: 50.5 us -> 0 us
  local copies, waits for them, and re-layouts: 32.3 us -> 0 us
  starting transfers between devices: 30.6 us -> 0 us
  waiting for transfers between devices: 16.7 us -> 0 us
  other arithmetic: 16.4 us -> 0 us
    psum x2 -> x0, blocking collectives: 210 us -> none  [body(): totals = lax.psum((scores, jnp.sum(bg_share)), ('tm', 'region'))]
    another operation x4 -> x0, loops' own time: 110 us -> none  [run_slots(): result = lax.fori_loop(0, PMAX, masked, initial)]
    pallas_call x0 -> x2, Pallas kernels: none -> 54.9 us  [the longest x1 53.6 us: body(): pl.pallas_call(lambda *refs: kernel(n_tm, n_region, *refs), out_shape=[pl...]
    dot_general x30 -> x0, matrix products: 50.5 us -> none  [the longest x18 27.6 us: excitation(): jnp.einsum('kl,lij->kij', mixture, spatial, precision=lax.Precision.HIGHEST)]
    ppermute x10 -> x0, starting transfers between devices: 30.6 us -> none  [the longest x8 20.4 us: shifted(): return lax.ppermute(block, axis, route)]
    dynamic_slice x96 -> x0, local copies, waits for them, and re-layouts: 30.5 us -> none  [the longest x24 15 us: fetch_pair(): candidate = source_list[slot_index]]
    ppermute x10 -> x0, waiting for transfers between devices: 16.7 us -> none  [the longest x8 15.6 us: shifted(): return lax.ppermute(block, axis, route)]
  transfers between devices with their start and end apart: 10 -> 0, of which waited for: 7 -> 0; matrix products, arithmetic and copies ran while one was open for 0% -> 0% of each run, Pallas kernels for 0% -> 0%
where the time goes in v1:
time: 57 us; the launch traced here: 56.8 us
  Pallas kernels  54.9 us (96%)
  between operations  1.93 us (3%)
    pallas_call x1, Pallas kernels, body(): pl.pallas_call(lambda *refs: kernel(n_tm, n_region, *refs), out_shape=[pl...  53.6 us
    pallas_call x1, Pallas kernels, body(): pl.pallas_call(finish, out_shape=results, in_specs=[vmem] * 4, out_specs=...  1.28 us

profile of v1, /device:TPU:1, one launch (start us, length us, event | category | flops | bytes accessed | tf_op | source)
XLA Modules:
  0.0 56.8 jit_solution(9104900209840288223)
XLA Ops:
  1.9 53.6 %etas_em.1 = (f32[16,16]{1,0:T(8,128)S(1)}, f32[1,1]{1,0:T(1,128)}, f32[24,128]{1,0:T(8,128)S(1)}, f32[24,128]{1,0:T(8,128)S(1)}) custom-call(f32[24,4,128]{2,1,0:T(4,128)} %bitcast.7, f32[24,128]{1,0:T(8,128)} %bitcast.8, f32[16]{0:T(128)} %refs_2_.1, f32[16]{0:T(128)} %refs_3_.1, f32[16,16]{1,0:T(8,128)} %refs_4_.1, f32[1]{0:T(128)S(6)} %copy.13.refs_5_, ...), custom_call_target="tpu_custom_call" | custom-call | tf_op jit(solution)/shard_map/etas_em/pallas_call | solution.py:464
  55.5 1.3 %hand_on.1 = (f32[16,16]{1,0:T(8,128)}, f32[1,1]{1,0:T(1,128)}, f32[24,128]{1,0:T(8,128)}, f32[24,128]{1,0:T(8,128)}) custom-call(f32[16,16]{1,0:T(8,128)S(1)} %get-tuple-element.12.refs_0_, f32[1,1]{1,0:T(1,128)} %get-tuple-element.13.refs_1_, f32[24,128]{1,0:T(8,128)S(1)} %get-tuple-element.14.refs_2_, f32[24,128]{1,0:T(8,128)S(1)} %get-tuple-element.15.refs_3_), custom_call_target="tpu_custom_call" | custom-call | tf_op jit(solution)/shard_map/hand_on/pallas_call | solution.py:517

commit v2 on v1

v2 whole, which is shorter than its diff:
```python
import math

import jax
import jax.numpy as jnp
from jax import lax
from jax.experimental import pallas as pl
from jax.experimental.pallas import tpu as pltpu
from jax.sharding import PartitionSpec as P

NK = 16
NL = 16
BLK = 128
NBLK = 24
DEPTH = 4
PMAX = 6
ITERS = 2
CELL = 3 * NBLK
NEAR = 3 * DEPTH - 1
PART = 80
RING = 8
FAR = 1.0e6
MESH = pl.DeviceIdType.MESH
PRODUCTIVITY = 1.0


def split_bf16(value):
    high = value.astype(jnp.bfloat16)
    low = (value - high.astype(jnp.float32)).astype(jnp.bfloat16)
    return high, low


def stacked_rows(value):
    high, low = split_bf16(value)
    return jnp.concatenate(
        [
            jnp.concatenate([high, high], axis=1),
            jnp.concatenate([low, jnp.zeros_like(low)], axis=1),
        ],
        axis=0,
    )


def spread_columns(ref, rows):
    for c in range(3):
        tile = jnp.concatenate([row[c : c + 1] for row in rows] + [rows[0][c : c + 1]] * (8 - len(rows)), axis=0)
        turned = jnp.transpose(tile)
        for p in range(len(rows)):
            ref[p, c] = jnp.broadcast_to(turned[:, p : p + 1], (BLK, BLK))


def columns(*rows):
    return jnp.transpose(jnp.concatenate(rows, axis=0))


def kernel(
    n_tm,
    n_region,
    ev_in,
    bg_in,
    decays_in,
    widths_in,
    mix_in,
    rate_s,
    block_in,
    source_in,
    count_s,
    mix_out,
    rate_out,
    share_out,
    offspring_out,
    bg_ref,
    decays_s,
    widths_s,
    mix_ref,
    block_s,
    source_s,
    events,
    beside,
    request,
    requests,
    cells,
    answer,
    picked,
    targets,
    sources,
    target_cols,
    source_cols,
    falloff,
    stats,
    early,
    late,
    coeff,
    payload_first,
    payload_last,
    partial_first,
    partial_last,
    returned,
    local_sem,
    request_send,
    request_recv,
    event_send,
    event_recv,
    answer_send,
    answer_recv,
    return_send,
    return_recv,
    sum_send,
    sum_recv,
):
    slab = lax.axis_index("tm")
    zone = lax.axis_index("region")
    events_all = float(n_tm * n_region * NBLK * BLK)
    payloads, partials = (payload_first, payload_last), (partial_first, partial_last)
    my_place = (zone, slab)

    def wrapped(place, step, length):
        moved = place + step
        return jnp.where(moved >= length, moved - length, jnp.where(moved < 0, moved + length, moved))

    def device(lag, side):
        return (wrapped(slab, lag, n_tm), wrapped(zone, side, n_region))

    x, z = lax.div(slab, RING), lax.div(zone, 2)
    y, core = slab - x * RING, zone - z * 2
    xs, zs = n_tm // RING, n_region // 2

    def hops(*steps):
        return -sum(min(step, length - step) for step, length in steps)

    row = sorted(
        ((dz, dc) for dz in range(zs) for dc in range(2) if dz or dc),
        key=lambda step: hops((step[0], zs)),
    )
    column = sorted(
        ((dx, dy) for dx in range(xs) for dy in range(RING) if dx or dy),
        key=lambda step: hops((step[0], xs), (step[1], RING)),
    )
    peers = (
        [(slab, wrapped(z, dz, zs) * 2 + wrapped(core, dc, 2)) for dz, dc in row],
        [(wrapped(x, dx, xs) * RING + wrapped(y, dy, RING), zone) for dx, dy in column],
    )

    staged = (
        (source_in, source_s),
        (block_in, block_s),
        (decays_in, decays_s),
        (widths_in, widths_s),
        (mix_in, mix_ref),
        (bg_in, bg_ref),
        (ev_in, events),
    )
    staging = [
        pltpu.make_async_copy(src, dst, local_sem.at[index])
        for index, (src, dst) in enumerate(staged)
    ]
    for copy in staging:
        copy.start()

    barrier = pltpu.get_barrier_semaphore()
    near = [(lag, 0) for lag in range(1, DEPTH)]
    near += [(lag, side) for lag in range(DEPTH) for side in (-1, 1)]
    greeted = [(-lag, side) for lag, side in near] + [(lag, -side) for lag, side in near if lag]
    greeted += [(0, step) for step in range(2, n_region - 1)]
    greeted += [(step, 0) for step in range(DEPTH, n_tm - DEPTH + 1)]
    for place in greeted:
        pl.semaphore_signal(barrier, inc=1, device_id=device(*place), device_id_type=MESH)
    staging[0].wait()
    row8 = lax.broadcasted_iota(jnp.int32, (8, BLK), 0)
    asked = jnp.zeros((8, BLK), jnp.int32)
    for p in range(PMAX):
        asked = jnp.where(row8 == p, source_s[0, 0, p], asked)
    request[...] = asked
    pl.semaphore_wait(barrier, len(greeted))

    pending = []

    def send(src, dst, send_sem, recv_sem, device):
        copy = pltpu.make_async_remote_copy(
            src_ref=src,
            dst_ref=dst,
            send_sem=send_sem,
            recv_sem=recv_sem,
            device_id=device,
            device_id_type=MESH,
        )
        copy.start()
        pending.append(copy)
        return copy

    def ask(index):
        lag, side = near[index]
        return send(
            request,
            requests.at[index],
            request_send.at[index],
            request_recv.at[index],
            device(-lag, side),
        )

    askers = DEPTH - 1
    request_copies = [ask(index) for index in range(askers)]

    staging[-1].wait()
    event_copies = [
        send(
            events,
            beside.at[side],
            event_send.at[side],
            event_recv.at[side],
            device(0, 1 - 2 * side),
        )
        for side in range(2)
    ]
    for copy in staging[1:-1]:
        copy.wait()
    decay_col = jnp.zeros((NK, BLK), jnp.float32)
    row16 = lax.broadcasted_iota(jnp.int32, (NK, BLK), 0)
    for k in range(NK):
        decay_col = jnp.where(row16 == k, decays_s[k], decay_col)
    width_col = jnp.zeros((NL, BLK), jnp.float32)
    for l in range(NL):
        width_col = jnp.where(row16 == l, widths_s[l], width_col)
    spread = 2.0 * width_col * width_col
    coeff[0] = -math.log2(math.e) / spread
    coeff[1] = 1.0 / (math.pi * spread)
    mix_tile = mix_ref[...]
    mixture = [jnp.broadcast_to(mix_tile[:, l : l + 1], (NK, BLK)) for l in range(NL)]
    mixture = jnp.concatenate(mixture, axis=0)
    own_yield = jnp.sum(jnp.exp(PRODUCTIVITY * events[:, 3, :]), axis=0, keepdims=True)
    own_yield = jnp.broadcast_to(jnp.sum(own_yield, axis=1, keepdims=True), (1, BLK))

    start_time = slab.astype(jnp.float32)
    live_count = count_s[0, 0]
    own_targets = [events[block_s[0, 0, p]] for p in range(PMAX)]
    for p, rows in enumerate(own_targets):
        targets[p] = rows
        live = jnp.where(p < live_count, 1.0, 0.0)
        late[p] = decay_col * jnp.exp(-decay_col * (rows[0:1] - start_time)) * live
    spread_columns(target_cols, own_targets)

    lane = lax.broadcasted_iota(jnp.int32, (8, 2 * BLK), 1)
    cell = jnp.where(lane >= 2 * PART, lane - 2 * PART, jnp.where(lane >= PART, lane - PART, lane))
    cell = jnp.where(lane >= 3 * PART, -1, cell)

    def one_hot(tile, lag):
        named = jnp.concatenate([tile, tile], axis=1) - lag * CELL
        return jnp.where(named == cell, 1.0, 0.0)

    for copy in event_copies:
        copy.wait_recv()
    for c in range(4):
        value = jnp.concatenate(
            [
                beside[0, :, c, :],
                events[:, c, :],
                beside[1, :, c, :],
                jnp.zeros((PART - CELL, BLK), jnp.float32),
            ],
            axis=0,
        )
        at = slice(c * BLK, (c + 1) * BLK)
        for part in range(3):
            term = value.astype(jnp.bfloat16)
            cells[part * PART : (part + 1) * PART, at] = term
            value = value - term.astype(jnp.float32)
        cells[3 * PART :, at] = jnp.zeros((2 * BLK - 3 * PART, BLK), jnp.bfloat16)
    for copy in request_copies:
        copy.wait_recv()
    wanted = [one_hot(asked, 0)] + [one_hot(requests[lag - 1], lag) for lag in range(1, DEPTH)]
    wanted = jnp.concatenate(wanted, axis=0).astype(jnp.bfloat16)
    found = jnp.dot(wanted, cells[...], preferred_element_type=jnp.float32)
    answer_copies = []
    for lag in range(DEPTH - 1, -1, -1):
        place = picked.at[0] if lag == 0 else answer.at[lag - 1]
        for c in range(4):
            place[c] = found[8 * lag : 8 * lag + 8, c * BLK : (c + 1) * BLK]
        if lag:
            answer_copies.append(
                send(
                    place,
                    picked.at[lag],
                    answer_send.at[lag - 1],
                    answer_recv.at[lag - 1],
                    device(lag, 0),
                )
            )
    for copy in answer_copies:
        copy.wait_recv()
    chosen = []
    for c in range(4):
        tile = picked[0, c]
        for lag in range(1, DEPTH):
            tile = jnp.where(asked >= lag * CELL, picked[lag, c], tile)
        chosen.append(tile)
    own_sources = [
        jnp.concatenate([chosen[c][p : p + 1] for c in range(4)], axis=0) for p in range(PMAX)
    ]
    for p, rows in enumerate(own_sources):
        sources[p] = rows
        early[p] = jnp.exp(decay_col * (rows[0:1] - start_time)) * jnp.exp(PRODUCTIVITY * rows[3:4])
    for c in range(3):
        turned = jnp.transpose(chosen[c])
        for p in range(PMAX):
            source_cols[p, c] = jnp.broadcast_to(turned[:, p : p + 1], (BLK, BLK))

    def distances(target, source):
        gap_time = target[0] - source[0]
        gap_east = target[1] - source[1]
        gap_north = target[2] - source[2]
        square = gap_east * gap_east + gap_north * gap_north
        return jnp.where(gap_time > 0.0, square, FAR)

    def as_rows(value):
        return [value[c : c + 1] for c in range(3)]

    def fall(square, l):
        return split_bf16(jnp.exp2(square * coeff[0, l : l + 1, :]))

    def prepare(index, carry):
        for p in (2 * index, 2 * index + 1):
            after = late[p]
            left = stacked_rows(early[p])
            square = distances(as_rows(targets[p]), [source_cols[p, c] for c in range(3)])
            for pair in range(NL // 2):
                parts = [
                    jnp.concatenate(fall(square, l), axis=0) for l in (2 * pair, 2 * pair + 1)
                ]
                right = jnp.concatenate(parts, axis=1)
                both = jnp.dot(left, right, preferred_element_type=jnp.float32)
                both = both[:NK] + both[NK:]
                for side in range(2):
                    l = 2 * pair + side
                    stats[p, l * NK : (l + 1) * NK, :] = (
                        both[:, side * BLK : (side + 1) * BLK] * after * coeff[1, l : l + 1, :]
                    )
        return carry

    lax.fori_loop(0, PMAX // 2, prepare, 0)

    def prepare_back(index, carry):
        for p in (2 * index, 2 * index + 1):
            square = distances([target_cols[p, c] for c in range(3)], as_rows(sources[p]))
            for l in range(NL):
                falloff[p, l, 0], falloff[p, l, 1] = fall(square, l)
        return carry

    block_row = lax.broadcasted_iota(jnp.int32, (NBLK, BLK), 0)
    background = bg_ref[...]

    def expect(mixture, rate):
        triggered = jnp.zeros((NBLK, BLK), jnp.float32)
        for p in range(PMAX):
            row = jnp.sum(stats[p] * mixture, axis=0, keepdims=True)
            triggered = triggered + jnp.where(block_row == block_s[0, 0, p], row, 0.0)
        level = rate * background
        inverse = 1.0 / (level + triggered)
        share = level * inverse
        weights = [
            jnp.sum(jnp.where(block_row == block_s[0, 0, p], inverse, 0.0), axis=0, keepdims=True)
            for p in range(PMAX)
        ]
        scores = stats[0] * weights[0]
        for p in range(1, PMAX):
            scores = scores + stats[p] * weights[p]
        rows = [
            jnp.sum(jnp.transpose(scores[half * BLK : (half + 1) * BLK]), axis=0, keepdims=True)
            for half in range(2)
        ]
        return share, weights, rows

    def start_sum(stage, value):
        sweep, axis = divmod(stage, 2)
        payload, partial = payloads[sweep].at[axis], partials[sweep].at[axis]
        payload[...] = value
        partial[my_place[axis]] = value
        for other in peers[axis]:
            pltpu.make_async_remote_copy(
                src_ref=payload,
                dst_ref=partial.at[my_place[axis]],
                send_sem=sum_send.at[stage],
                recv_sem=sum_recv.at[stage],
                device_id=other,
                device_id_type=MESH,
            ).start()

    def others(stage, sems):
        sweep, axis = divmod(stage, 2)
        part = partials[sweep].at[axis, pl.ds(0, len(peers[axis]))]
        return pltpu.make_async_copy(part, part, sems.at[stage])

    def end_sum(stage):
        sweep, axis = divmod(stage, 2)
        others(stage, sum_recv).wait()
        return jnp.sum(partials[sweep][axis, 0 : len(peers[axis]) + 1], axis=0)

    def update(mixture, total, yield_total):
        cols = columns(*([total] * (8 // total.shape[0])))
        factor = jnp.concatenate(
            [jnp.broadcast_to(cols[:, half : half + 1], (BLK, BLK)) for half in range(2)], axis=0
        )
        mass = mixture * factor
        triggered = jnp.sum(mass, axis=0, keepdims=True)
        return mass / yield_total, 1.0 - triggered / events_all

    share, weights, rows = expect(mixture, jnp.full((1, BLK), rate_s[0], jnp.float32))
    value = jnp.concatenate(rows + [own_yield, own_yield], axis=0)
    start_sum(0, value)
    request_copies = [ask(index) for index in range(askers, len(near))]
    lax.fori_loop(0, 2, prepare_back, 0)
    value = end_sum(0)
    start_sum(1, value)
    lax.fori_loop(2, 3, prepare_back, 0)
    for copy in request_copies:
        copy.wait_recv()
    for copy in pending:
        copy.wait_send()
    pending.clear()
    value = end_sum(1)
    yield_total = value[2:3, :]
    mixture, rate = update(mixture, value, yield_total)

    share, weights, rows = expect(mixture, rate)
    start_sum(2, jnp.concatenate(rows, axis=0))
    share_out[...] = share
    scaled = mixture * jnp.concatenate(
        [jnp.broadcast_to(coeff[1, l : l + 1, :], (NK, BLK)) for l in range(NL)], axis=0
    )

    for p in range(PMAX):
        late[p] = late[p] * weights[p]

    stats[0] = scaled

    def give_back(index, rows):
        for p in (2 * index, 2 * index + 1):
            left = stacked_rows(late[p])
            gathered = jnp.zeros((NK, BLK), jnp.float32)
            for pair in range(NL // 2):
                right = jnp.concatenate(
                    [
                        jnp.concatenate([falloff[p, l, 0], falloff[p, l, 1]], axis=0)
                        for l in (2 * pair, 2 * pair + 1)
                    ],
                    axis=1,
                )
                both = jnp.dot(left, right, preferred_element_type=jnp.float32)
                both = both[:NK] + both[NK:]
                for side in range(2):
                    l = 2 * pair + side
                    gathered = (
                        gathered
                        + both[:, side * BLK : (side + 1) * BLK] * stats[0, l * NK : (l + 1) * NK, :]
                    )
            row = jnp.sum(gathered * early[p], axis=0, keepdims=True)
            rows = jnp.where(lax.broadcasted_iota(jnp.int32, (8, BLK), 0) == p, row, rows)
        return rows

    rows = lax.fori_loop(0, PMAX // 2, give_back, jnp.zeros((8, BLK), jnp.float32))
    returned[0] = rows
    return_copies = [
        send(
            returned.at[0],
            returned.at[index + 1],
            return_send.at[index],
            return_recv.at[index],
            device(-lag, side),
        )
        for index, (lag, side) in enumerate(near)
    ]
    value = end_sum(2)
    start_sum(3, value)

    for copy in return_copies:
        copy.wait_recv()
    gathered = jnp.zeros((NBLK, BLK), jnp.float32)
    for index, (lag, side) in enumerate([(0, 0)] + near):
        first = (lag * 3 + side + 1) * NBLK
        for p in range(PMAX):
            named = asked[p : p + 1] if index == 0 else requests[index - 1, p : p + 1, :]
            gathered = gathered + jnp.where(
                block_row == named - first, returned[index, p : p + 1, :], 0.0
            )
    offspring_out[...] = gathered
    for copy in pending:
        copy.wait_send()
    for stage in range(3):
        others(stage, sum_send).wait()
    value = end_sum(3)
    others(3, sum_send).wait()
    mixture, rate = update(mixture, value, yield_total)
    lane16 = lax.broadcasted_iota(jnp.int32, (NK, BLK), 1)
    square_mix = jnp.zeros((NK, BLK), jnp.float32)
    for l in range(NL):
        square_mix = jnp.where(lane16 == l, mixture[l * NK : (l + 1) * NK], square_mix)
    mix_out[...] = square_mix[:, :NL]
    rate_out[...] = rate[:, 0:1]


def finish(*refs):
    arrived, handed, sems = refs[:4], refs[4:8], refs[8]
    copies = [
        pltpu.make_async_copy(src, dst, sems.at[index])
        for index, (src, dst) in enumerate(zip(arrived, handed))
    ]
    for copy in copies:
        copy.start()
    for copy in copies:
        copy.wait()


def solution(mesh):
    n_tm, n_region = mesh.shape["tm"], mesh.shape["region"]

    def body(
        events, background, decays, widths, mix_start, rate_start, pair_block, pair_source, pair_count
    ):
        blocks = jnp.transpose(jnp.reshape(events, (4, NBLK, BLK)), (1, 0, 2))
        smem = pl.BlockSpec(memory_space=pltpu.SMEM)
        hbm = pl.BlockSpec(memory_space=pltpu.HBM)
        vmem = pl.BlockSpec(memory_space=pltpu.VMEM)
        f32 = jnp.float32
        dma = pltpu.SemaphoreType.DMA
        results = [
            jax.ShapeDtypeStruct((NK, NL), f32),
            jax.ShapeDtypeStruct((1, 1), f32),
            jax.ShapeDtypeStruct((NBLK, BLK), f32),
            jax.ShapeDtypeStruct((NBLK, BLK), f32),
        ]
        found = pl.pallas_call(
            lambda *refs: kernel(n_tm, n_region, *refs),
            out_shape=[pltpu.VMEM(leaf.shape, leaf.dtype) for leaf in results],
            in_specs=[hbm] * 5 + [smem, hbm, hbm, smem],
            out_specs=[vmem] * 4,
            scratch_shapes=[
                pltpu.VMEM((NBLK, BLK), f32),
                pltpu.SMEM(decays.shape, f32),
                pltpu.SMEM(widths.shape, f32),
                pltpu.VMEM(mix_start.shape, f32),
                pltpu.SMEM(pair_block.shape, jnp.int32),
                pltpu.SMEM(pair_source.shape, jnp.int32),
                pltpu.VMEM((NBLK, 4, BLK), f32),
                pltpu.VMEM((2, NBLK, 4, BLK), f32),
                pltpu.VMEM((8, BLK), jnp.int32),
                pltpu.VMEM((NEAR, 8, BLK), jnp.int32),
                pltpu.VMEM((2 * BLK, 4 * BLK), jnp.bfloat16),
                pltpu.VMEM((DEPTH - 1, 4, 8, BLK), f32),
                pltpu.VMEM((DEPTH, 4, 8, BLK), f32),
                pltpu.VMEM((PMAX, 4, BLK), f32),
                pltpu.VMEM((PMAX, 4, BLK), f32),
                pltpu.VMEM((PMAX, 3, BLK, BLK), f32),
                pltpu.VMEM((PMAX, 3, BLK, BLK), f32),
                pltpu.VMEM((PMAX, NL, 2, BLK, BLK), jnp.bfloat16),
                pltpu.VMEM((PMAX, NK * NL, BLK), f32),
                pltpu.VMEM((PMAX, NK, BLK), f32),
                pltpu.VMEM((PMAX, NK, BLK), f32),
                pltpu.VMEM((2, NL, BLK), f32),
                pltpu.VMEM((2, 4, BLK), f32),
                pltpu.VMEM((2, 2, BLK), f32),
                pltpu.VMEM((2, max(n_tm, n_region), 4, BLK), f32),
                pltpu.VMEM((2, max(n_tm, n_region), 2, BLK), f32),
                pltpu.VMEM((NEAR + 1, 8, BLK), f32),
                dma((7,)),
                dma((NEAR,)),
                dma((NEAR,)),
                dma((2,)),
                dma((2,)),
                dma((DEPTH - 1,)),
                dma((DEPTH - 1,)),
                dma((NEAR,)),
                dma((NEAR,)),
                dma((2 * ITERS,)),
                dma((2 * ITERS,)),
            ],
            compiler_params=pltpu.CompilerParams(
                collective_id=0, has_side_effects=True, vmem_limit_bytes=60 * 2**20
            ),
            name="etas_em",
        )(
            blocks,
            jnp.reshape(background, (NBLK, BLK)),
            decays,
            widths,
            mix_start,
            rate_start,
            pair_block,
            pair_source,
            pair_count,
        )
        mixture, rate, share, offspring = pl.pallas_call(
            finish,
            out_shape=results,
            in_specs=[vmem] * 4,
            out_specs=[hbm] * 4,
            scratch_shapes=[dma((4,))],
            compiler_params=pltpu.CompilerParams(vmem_limit_bytes=2**20),
            name="hand_on",
        )(*found)
        return (
            mixture,
            jnp.reshape(rate, (1,)),
            jnp.reshape(share, (1, 1, NBLK * BLK)),
            jnp.reshape(offspring, (1, 1, NBLK * BLK)),
        )

    placed = (
        P("tm", "region", None, None),
        P("tm", "region", None),
        P(),
        P(),
        P(),
        P(),
        P("tm", "region", None),
        P("tm", "region", None),
        P("tm", "region"),
    )
    return jax.shard_map(
        body,
        mesh=mesh,
        in_specs=placed,
        out_specs=(P(), P(), P("tm", "region", None), P("tm", "region", None)),
        check_vma=False,
    )
```

time: 57 us -> 55.2 us (0.968)
  Pallas kernels: 54.9 us -> 53.1 us
    pallas_call x1, Pallas kernels: 53.6 us -> 51.8 us  [body(): pl.pallas_call(lambda *refs: kernel(n_tm, n_region, *refs), out_shape=[pl...]
where the time goes in v2:
time: 55.2 us; the launch traced here: 55.1 us
  Pallas kernels  53.1 us (96%)
  between operations  1.93 us (3%)
    pallas_call x1, Pallas kernels, body(): pl.pallas_call(lambda *refs: kernel(n_tm, n_region, *refs), out_shape=[pl...  51.8 us
    pallas_call x1, Pallas kernels, body(): pl.pallas_call(finish, out_shape=results, in_specs=[vmem] * 4, out_specs=...  1.28 us

profile of v2, /device:TPU:1, one launch (start us, length us, event | category | flops | bytes accessed | tf_op | source)
XLA Modules:
  0.0 55.1 jit_solution(8580647095962811169)
XLA Ops:
  1.9 51.8 %etas_em.1 = (f32[16,16]{1,0:T(8,128)S(1)}, f32[1,1]{1,0:T(1,128)}, f32[24,128]{1,0:T(8,128)S(1)}, f32[24,128]{1,0:T(8,128)S(1)}) custom-call(f32[24,4,128]{2,1,0:T(4,128)} %bitcast.7, f32[24,128]{1,0:T(8,128)} %bitcast.8, f32[16]{0:T(128)} %refs_2_.1, f32[16]{0:T(128)} %refs_3_.1, f32[16,16]{1,0:T(8,128)} %refs_4_.1, f32[1]{0:T(128)S(6)} %copy.13.refs_5_, ...), custom_call_target="tpu_custom_call" | custom-call | tf_op jit(solution)/shard_map/etas_em/pallas_call | solution.py:529
  53.8 1.3 %hand_on.1 = (f32[16,16]{1,0:T(8,128)}, f32[1,1]{1,0:T(1,128)}, f32[24,128]{1,0:T(8,128)}, f32[24,128]{1,0:T(8,128)}) custom-call(f32[16,16]{1,0:T(8,128)S(1)} %get-tuple-element.12.refs_0_, f32[1,1]{1,0:T(1,128)} %get-tuple-element.13.refs_1_, f32[24,128]{1,0:T(8,128)S(1)} %get-tuple-element.14.refs_2_, f32[24,128]{1,0:T(8,128)S(1)} %get-tuple-element.15.refs_3_), custom_call_target="tpu_custom_call" | custom-call | tf_op jit(solution)/shard_map/hand_on/pallas_call | solution.py:589

commit v3 on v2

--- a/solution.py
+++ b/solution.py
@@ -84,7 +84,6 @@
     targets,
     sources,
     target_cols,
-    source_cols,
     falloff,
     stats,
     early,
@@ -111,7 +110,6 @@
     zone = lax.axis_index("region")
     events_all = float(n_tm * n_region * NBLK * BLK)
     payloads, partials = (payload_first, payload_last), (partial_first, partial_last)
-    my_place = (zone, slab)
 
     def wrapped(place, step, length):
         moved = place + step
@@ -128,17 +126,18 @@
         return -sum(min(step, length - step) for step, length in steps)
 
     row = sorted(
-        ((dz, dc) for dz in range(zs) for dc in range(2) if dz or dc),
-        key=lambda step: hops((step[0], zs)),
+        ((dy, dc) for dy in range(RING) for dc in range(2) if dy or dc),
+        key=lambda step: hops((step[0], RING)),
     )
     column = sorted(
-        ((dx, dy) for dx in range(xs) for dy in range(RING) if dx or dy),
-        key=lambda step: hops((step[0], xs), (step[1], RING)),
+        ((dx, dz) for dx in range(xs) for dz in range(zs) if dx or dz),
+        key=lambda step: hops((step[0], xs), (step[1], zs)),
     )
     peers = (
-        [(slab, wrapped(z, dz, zs) * 2 + wrapped(core, dc, 2)) for dz, dc in row],
-        [(wrapped(x, dx, xs) * RING + wrapped(y, dy, RING), zone) for dx, dy in column],
-    )
+        [(x * RING + wrapped(y, dy, RING), z * 2 + wrapped(core, dc, 2)) for dy, dc in row],
+        [(wrapped(x, dx, xs) * RING + y, wrapped(z, dz, zs) * 2 + core) for dx, dz in column],
+    )
+    my_place = (y * 2 + core, x * zs + z)
 
     staged = (
         (source_in, source_s),
@@ -159,11 +158,17 @@
     barrier = pltpu.get_barrier_semaphore()
     near = [(lag, 0) for lag in range(1, DEPTH)]
     near += [(lag, side) for lag in range(DEPTH) for side in (-1, 1)]
-    greeted = [(-lag, side) for lag, side in near] + [(lag, -side) for lag, side in near if lag]
-    greeted += [(0, step) for step in range(2, n_region - 1)]
-    greeted += [(step, 0) for step in range(DEPTH, n_tm - DEPTH + 1)]
-    for place in greeted:
-        pl.semaphore_signal(barrier, inc=1, device_id=device(*place), device_id_type=MESH)
+    greeted = [
+        (hops((step[0], RING)), place) for step, place in zip(row, peers[0])
+    ] + [
+        (hops((step[0], xs), (step[1], zs)), place) for step, place in zip(column, peers[1])
+    ]
+    for lag, side in near:
+        greeted.append((-lag - abs(side), device(-lag, side)))
+        if lag:
+            greeted.append((-lag - abs(side), device(lag, -side)))
+    for _, place in sorted(greeted, key=lambda entry: entry[0]):
+        pl.semaphore_signal(barrier, inc=1, device_id=place, device_id_type=MESH)
     staging[0].wait()
     row8 = lax.broadcasted_iota(jnp.int32, (8, BLK), 0)
     asked = jnp.zeros((8, BLK), jnp.int32)
@@ -272,8 +277,9 @@
     answer_copies = []
     for lag in range(DEPTH - 1, -1, -1):
         place = picked.at[0] if lag == 0 else answer.at[lag - 1]
-        for c in range(4):
-            place[c] = found[8 * lag : 8 * lag + 8, c * BLK : (c + 1) * BLK]
+        place[...] = jnp.concatenate(
+            [found[8 * lag : 8 * lag + PMAX, c * BLK : (c + 1) * BLK] for c in range(4)], axis=0
+        )
         if lag:
             answer_copies.append(
                 send(
@@ -284,24 +290,17 @@
                     device(lag, 0),
                 )
             )
+    asked_rows = jnp.concatenate([asked[:PMAX]] * 4, axis=0)
     for copy in answer_copies:
         copy.wait_recv()
-    chosen = []
-    for c in range(4):
-        tile = picked[0, c]
-        for lag in range(1, DEPTH):
-            tile = jnp.where(asked >= lag * CELL, picked[lag, c], tile)
-        chosen.append(tile)
-    own_sources = [
-        jnp.concatenate([chosen[c][p : p + 1] for c in range(4)], axis=0) for p in range(PMAX)
-    ]
-    for p, rows in enumerate(own_sources):
-        sources[p] = rows
-        early[p] = jnp.exp(decay_col * (rows[0:1] - start_time)) * jnp.exp(PRODUCTIVITY * rows[3:4])
-    for c in range(3):
-        turned = jnp.transpose(chosen[c])
-        for p in range(PMAX):
-            source_cols[p, c] = jnp.broadcast_to(turned[:, p : p + 1], (BLK, BLK))
+    chosen = picked[0]
+    for lag in range(1, DEPTH):
+        chosen = jnp.where(asked_rows >= lag * CELL, picked[lag], chosen)
+    turned = jnp.transpose(chosen)
+    for p in range(PMAX):
+        rows = [chosen[c * PMAX + p : c * PMAX + p + 1] for c in range(4)]
+        sources[p] = jnp.concatenate(rows, axis=0)
+        early[p] = jnp.exp(decay_col * (rows[0] - start_time)) * jnp.exp(PRODUCTIVITY * rows[3])
 
     def distances(target, source):
         gap_time = target[0] - source[0]
@@ -316,26 +315,26 @@
     def fall(square, l):
         return split_bf16(jnp.exp2(square * coeff[0, l : l + 1, :]))
 
-    def prepare(index, carry):
-        for p in (2 * index, 2 * index + 1):
-            after = late[p]
-            left = stacked_rows(early[p])
-            square = distances(as_rows(targets[p]), [source_cols[p, c] for c in range(3)])
-            for pair in range(NL // 2):
-                parts = [
-                    jnp.concatenate(fall(square, l), axis=0) for l in (2 * pair, 2 * pair + 1)
-                ]
-                right = jnp.concatenate(parts, axis=1)
-                both = jnp.dot(left, right, preferred_element_type=jnp.float32)
-                both = both[:NK] + both[NK:]
-                for side in range(2):
-                    l = 2 * pair + side
-                    stats[p, l * NK : (l + 1) * NK, :] = (
-                        both[:, side * BLK : (side + 1) * BLK] * after * coeff[1, l : l + 1, :]
-                    )
-        return carry
-
-    lax.fori_loop(0, PMAX // 2, prepare, 0)
+    first_rows = []
+    for p in range(PMAX):
+        after = late[p]
+        left = stacked_rows(early[p])
+        square = distances(
+            as_rows(targets[p]),
+            [turned[:, c * PMAX + p : c * PMAX + p + 1] for c in range(3)],
+        )
+        summed = jnp.zeros((NK, BLK), jnp.float32)
+        for pair in range(NL // 2):
+            parts = [jnp.concatenate(fall(square, l), axis=0) for l in (2 * pair, 2 * pair + 1)]
+            right = jnp.concatenate(parts, axis=1)
+            both = jnp.dot(left, right, preferred_element_type=jnp.float32)
+            both = both[:NK] + both[NK:]
+            for side in range(2):
+                l = 2 * pair + side
+                tile = both[:, side * BLK : (side + 1) * BLK] * after * coeff[1, l : l + 1, :]
+                stats[p, l * NK : (l + 1) * NK, :] = tile
+                summed = summed + tile * mixture[l * NK : (l + 1) * NK]
+        first_rows.append(jnp.sum(summed, axis=0, keepdims=True))
 
     def prepare_back(index, carry):
         for p in (2 * index, 2 * index + 1):
@@ -347,10 +346,10 @@
     block_row = lax.broadcasted_iota(jnp.int32, (NBLK, BLK), 0)
     background = bg_ref[...]
 
-    def expect(mixture, rate):
+    def expect(row_of, rate):
         triggered = jnp.zeros((NBLK, BLK), jnp.float32)
         for p in range(PMAX):
-            row = jnp.sum(stats[p] * mixture, axis=0, keepdims=True)
+            row = row_of(p)
             triggered = triggered + jnp.where(block_row == block_s[0, 0, p], row, 0.0)
         level = rate * background
         inverse = 1.0 / (level + triggered)
@@ -400,9 +399,9 @@
         )
         mass = mixture * factor
         triggered = jnp.sum(mass, axis=0, keepdims=True)
-        return mass / yield_total, 1.0 - triggered / events_all
-
-    share, weights, rows = expect(mixture, jnp.full((1, BLK), rate_s[0], jnp.float32))
+        return mass * (1.0 / yield_total), 1.0 - triggered / events_all
+
+    share, weights, rows = expect(lambda p: first_rows[p], jnp.full((1, BLK), rate_s[0], jnp.float32))
     value = jnp.concatenate(rows + [own_yield, own_yield], axis=0)
     start_sum(0, value)
     request_copies = [ask(index) for index in range(askers, len(near))]
@@ -419,7 +418,9 @@
     yield_total = value[2:3, :]
     mixture, rate = update(mixture, value, yield_total)
 
-    share, weights, rows = expect(mixture, rate)
+    share, weights, rows = expect(
+        lambda p: jnp.sum(stats[p] * mixture, axis=0, keepdims=True), rate
+    )
     start_sum(2, jnp.concatenate(rows, axis=0))
     share_out[...] = share
     scaled = mixture * jnp.concatenate(
@@ -543,11 +544,10 @@
                 pltpu.VMEM((8, BLK), jnp.int32),
                 pltpu.VMEM((NEAR, 8, BLK), jnp.int32),
                 pltpu.VMEM((2 * BLK, 4 * BLK), jnp.bfloat16),
-                pltpu.VMEM((DEPTH - 1, 4, 8, BLK), f32),
-                pltpu.VMEM((DEPTH, 4, 8, BLK), f32),
+                pltpu.VMEM((DEPTH - 1, 4 * PMAX, BLK), f32),
+                pltpu.VMEM((DEPTH, 4 * PMAX, BLK), f32),
                 pltpu.VMEM((PMAX, 4, BLK), f32),
                 pltpu.VMEM((PMAX, 4, BLK), f32),
-                pltpu.VMEM((PMAX, 3, BLK, BLK), f32),
                 pltpu.VMEM((PMAX, 3, BLK, BLK), f32),
                 pltpu.VMEM((PMAX, NL, 2, BLK, BLK), jnp.bfloat16),
                 pltpu.VMEM((PMAX, NK * NL, BLK), f32),

time: 55.2 us -> 54.6 us (0.989)
  Pallas kernels: 53.1 us -> 52.5 us
    pallas_call x1, Pallas kernels: 51.8 us -> 51.2 us  [body(): pl.pallas_call(lambda *refs: kernel(n_tm, n_region, *refs), out_shape=[pl...]
where the time goes in v3:
time: 54.6 us; the launch traced here: 54.4 us
  Pallas kernels  52.5 us (96%)
  between operations  1.93 us (4%)
    pallas_call x1, Pallas kernels, body(): pl.pallas_call(lambda *refs: kernel(n_tm, n_region, *refs), out_shape=[pl...  51.2 us
    pallas_call x1, Pallas kernels, body(): pl.pallas_call(finish, out_shape=results, in_specs=[vmem] * 4, out_specs=...  1.28 us

profile of v3, /device:TPU:1, one launch (start us, length us, event | category | flops | bytes accessed | tf_op | source)
XLA Modules:
  0.0 54.4 jit_solution(12798428514536758695)
XLA Ops:
  1.9 51.2 %etas_em.1 = (f32[16,16]{1,0:T(8,128)S(1)}, f32[1,1]{1,0:T(1,128)}, f32[24,128]{1,0:T(8,128)S(1)}, f32[24,128]{1,0:T(8,128)S(1)}) custom-call(f32[24,4,128]{2,1,0:T(4,128)} %bitcast.7, f32[24,128]{1,0:T(8,128)} %bitcast.8, f32[16]{0:T(128)} %refs_2_.1, f32[16]{0:T(128)} %refs_3_.1, f32[16,16]{1,0:T(8,128)} %refs_4_.1, f32[1]{0:T(128)S(6)} %copy.13.refs_5_, ...), custom_call_target="tpu_custom_call" | custom-call | tf_op jit(solution)/shard_map/etas_em/pallas_call | solution.py:530
  53.1 1.3 %hand_on.1 = (f32[16,16]{1,0:T(8,128)}, f32[1,1]{1,0:T(1,128)}, f32[24,128]{1,0:T(8,128)}, f32[24,128]{1,0:T(8,128)}) custom-call(f32[16,16]{1,0:T(8,128)S(1)} %get-tuple-element.12.refs_0_, f32[1,1]{1,0:T(1,128)} %get-tuple-element.13.refs_1_, f32[24,128]{1,0:T(8,128)S(1)} %get-tuple-element.14.refs_2_, f32[24,128]{1,0:T(8,128)S(1)} %get-tuple-element.15.refs_3_), custom_call_target="tpu_custom_call" | custom-call | tf_op jit(solution)/shard_map/hand_on/pallas_call | solution.py:589

commit v4 on v3

--- a/solution.py
+++ b/solution.py
@@ -105,6 +105,7 @@
     return_recv,
     sum_send,
     sum_recv,
+    ready,
 ):
     slab = lax.axis_index("tm")
     zone = lax.axis_index("region")
@@ -158,24 +159,50 @@
     barrier = pltpu.get_barrier_semaphore()
     near = [(lag, 0) for lag in range(1, DEPTH)]
     near += [(lag, side) for lag in range(DEPTH) for side in (-1, 1)]
-    greeted = [
-        (hops((step[0], RING)), place) for step, place in zip(row, peers[0])
-    ] + [
-        (hops((step[0], xs), (step[1], zs)), place) for step, place in zip(column, peers[1])
-    ]
+    def inward(place, length):
+        return 2 * min(place, length - place) - (1 <= place <= length // 2)
+
+    def inward_of(place, length):
+        rank = 0
+        for other in range(1, length):
+            rank = jnp.where(place == other, inward(other, length), rank)
+        return rank
+
+    ranks = (2 * inward_of(y, RING) + 1 - core, xs * z + inward_of(x, xs))
+    by_rank = (
+        [
+            (2 * inward(oy, RING) + 1 - oc, (x * RING + oy, z * 2 + oc))
+            for oy in range(RING)
+            for oc in range(2)
+        ],
+        [
+            (xs * oz + inward(ox, xs), (ox * RING + y, oz * 2 + core))
+            for ox in range(xs)
+            for oz in range(zs)
+        ],
+    )
+
+    def greet(place):
+        pl.semaphore_signal(barrier, inc=1, device_id=place, device_id_type=MESH)
+
     for lag, side in near:
-        greeted.append((-lag - abs(side), device(-lag, side)))
+        greet(device(-lag, side))
         if lag:
-            greeted.append((-lag - abs(side), device(lag, -side)))
-    for _, place in sorted(greeted, key=lambda entry: entry[0]):
-        pl.semaphore_signal(barrier, inc=1, device_id=place, device_id_type=MESH)
+            greet(device(lag, -side))
+    for axis in range(2):
+        for rank, place in by_rank[axis]:
+
+            @pl.when(rank > ranks[axis])
+            def _():
+                greet(place)
+
     staging[0].wait()
     row8 = lax.broadcasted_iota(jnp.int32, (8, BLK), 0)
     asked = jnp.zeros((8, BLK), jnp.int32)
     for p in range(PMAX):
         asked = jnp.where(row8 == p, source_s[0, 0, p], asked)
     request[...] = asked
-    pl.semaphore_wait(barrier, len(greeted))
+    pl.semaphore_wait(barrier, 2 * len(near) - 2 + ranks[0] + ranks[1])
 
     pending = []
 
@@ -216,6 +243,15 @@
         )
         for side in range(2)
     ]
+    for axis in range(2):
+        for rank, place in by_rank[axis]:
+
+            @pl.when(rank < ranks[axis])
+            def _():
+                pl.semaphore_signal(
+                    ready.at[axis], inc=1, device_id=place, device_id_type=MESH
+                )
+
     for copy in staging[1:-1]:
         copy.wait()
     decay_col = jnp.zeros((NK, BLK), jnp.float32)
@@ -244,12 +280,10 @@
     spread_columns(target_cols, own_targets)
 
     lane = lax.broadcasted_iota(jnp.int32, (8, 2 * BLK), 1)
-    cell = jnp.where(lane >= 2 * PART, lane - 2 * PART, jnp.where(lane >= PART, lane - PART, lane))
-    cell = jnp.where(lane >= 3 * PART, -1, cell)
-
-    def one_hot(tile, lag):
-        named = jnp.concatenate([tile, tile], axis=1) - lag * CELL
-        return jnp.where(named == cell, 1.0, 0.0)
+
+    def one_hot(tile, lag, part):
+        named = jnp.concatenate([tile, tile], axis=1) - (lag * CELL - part * PART)
+        return jnp.where(named == lane, 1.0, 0.0)
 
     for copy in event_copies:
         copy.wait_recv()
@@ -271,9 +305,13 @@
         cells[3 * PART :, at] = jnp.zeros((2 * BLK - 3 * PART, BLK), jnp.bfloat16)
     for copy in request_copies:
         copy.wait_recv()
-    wanted = [one_hot(asked, 0)] + [one_hot(requests[lag - 1], lag) for lag in range(1, DEPTH)]
-    wanted = jnp.concatenate(wanted, axis=0).astype(jnp.bfloat16)
-    found = jnp.dot(wanted, cells[...], preferred_element_type=jnp.float32)
+    tiles = [asked] + [requests[lag - 1] for lag in range(1, DEPTH)]
+    wanted = jnp.concatenate(
+        [one_hot(tile, lag, part) for part in range(3) for lag, tile in enumerate(tiles)], axis=0
+    ).astype(jnp.bfloat16)
+    terms = jnp.dot(wanted, cells[...], preferred_element_type=jnp.float32)
+    rows = 8 * DEPTH
+    found = (terms[:rows] + terms[rows : 2 * rows]) + terms[2 * rows :]
     answer_copies = []
     for lag in range(DEPTH - 1, -1, -1):
         place = picked.at[0] if lag == 0 else answer.at[lag - 1]
@@ -369,6 +407,13 @@
 
     def start_sum(stage, value):
         sweep, axis = divmod(stage, 2)
+        if sweep == 0:
+            later = len(peers[axis]) - ranks[axis]
+
+            @pl.when(later > 0)
+            def _():
+                pl.semaphore_wait(ready.at[axis], later)
+
         payload, partial = payloads[sweep].at[axis], partials[sweep].at[axis]
         payload[...] = value
         partial[my_place[axis]] = value
@@ -570,6 +615,7 @@
                 dma((NEAR,)),
                 dma((2 * ITERS,)),
                 dma((2 * ITERS,)),
+                pltpu.SemaphoreType.REGULAR((2,)),
             ],
             compiler_params=pltpu.CompilerParams(
                 collective_id=0, has_side_effects=True, vmem_limit_bytes=60 * 2**20

time: 54.6 us -> 54.7 us (level)
  no operation moved by 1% of the time
where the time goes in v4:
time: 54.7 us; the launch traced here: 54.5 us
  Pallas kernels  52.6 us (96%)
  between operations  1.93 us (4%)
    pallas_call x1, Pallas kernels, body(): pl.pallas_call(lambda *refs: kernel(n_tm, n_region, *refs), out_shape=[pl...  51.3 us
    pallas_call x1, Pallas kernels, body(): pl.pallas_call(finish, out_shape=results, in_specs=[vmem] * 4, out_specs=...  1.28 us

profile of v4, /device:TPU:1, one launch (start us, length us, event | category | flops | bytes accessed | tf_op | source)
XLA Modules:
  0.0 54.5 jit_solution(9785661583019879681)
XLA Ops:
  1.9 51.3 %etas_em.1 = (f32[16,16]{1,0:T(8,128)S(1)}, f32[1,1]{1,0:T(1,128)}, f32[24,128]{1,0:T(8,128)S(1)}, f32[24,128]{1,0:T(8,128)S(1)}) custom-call(f32[24,4,128]{2,1,0:T(4,128)} %bitcast.7, f32[24,128]{1,0:T(8,128)} %bitcast.8, f32[16]{0:T(128)} %refs_2_.1, f32[16]{0:T(128)} %refs_3_.1, f32[16,16]{1,0:T(8,128)} %refs_4_.1, f32[1]{0:T(128)S(6)} %copy.13.refs_5_, ...), custom_call_target="tpu_custom_call" | custom-call | tf_op jit(solution)/shard_map/etas_em/pallas_call | solution.py:575
  53.2 1.3 %hand_on.1 = (f32[16,16]{1,0:T(8,128)}, f32[1,1]{1,0:T(1,128)}, f32[24,128]{1,0:T(8,128)}, f32[24,128]{1,0:T(8,128)}) custom-call(f32[16,16]{1,0:T(8,128)S(1)} %get-tuple-element.12.refs_0_, f32[1,1]{1,0:T(1,128)} %get-tuple-element.13.refs_1_, f32[24,128]{1,0:T(8,128)S(1)} %get-tuple-element.14.refs_2_, f32[24,128]{1,0:T(8,128)S(1)} %get-tuple-element.15.refs_3_), custom_call_target="tpu_custom_call" | custom-call | tf_op jit(solution)/shard_map/hand_on/pallas_call | solution.py:635

commit v5 on v3

--- a/solution.py
+++ b/solution.py
@@ -244,12 +244,10 @@
     spread_columns(target_cols, own_targets)
 
     lane = lax.broadcasted_iota(jnp.int32, (8, 2 * BLK), 1)
-    cell = jnp.where(lane >= 2 * PART, lane - 2 * PART, jnp.where(lane >= PART, lane - PART, lane))
-    cell = jnp.where(lane >= 3 * PART, -1, cell)
-
-    def one_hot(tile, lag):
-        named = jnp.concatenate([tile, tile], axis=1) - lag * CELL
-        return jnp.where(named == cell, 1.0, 0.0)
+
+    def one_hot(tile, lag, part):
+        named = jnp.concatenate([tile, tile], axis=1) - (lag * CELL - part * PART)
+        return jnp.where(named == lane, 1.0, 0.0)
 
     for copy in event_copies:
         copy.wait_recv()
@@ -271,9 +269,13 @@
         cells[3 * PART :, at] = jnp.zeros((2 * BLK - 3 * PART, BLK), jnp.bfloat16)
     for copy in request_copies:
         copy.wait_recv()
-    wanted = [one_hot(asked, 0)] + [one_hot(requests[lag - 1], lag) for lag in range(1, DEPTH)]
-    wanted = jnp.concatenate(wanted, axis=0).astype(jnp.bfloat16)
-    found = jnp.dot(wanted, cells[...], preferred_element_type=jnp.float32)
+    tiles = [asked] + [requests[lag - 1] for lag in range(1, DEPTH)]
+    wanted = jnp.concatenate(
+        [one_hot(tile, lag, part) for part in range(3) for lag, tile in enumerate(tiles)], axis=0
+    ).astype(jnp.bfloat16)
+    terms = jnp.dot(wanted, cells[...], preferred_element_type=jnp.float32)
+    rows = 8 * DEPTH
+    found = (terms[:rows] + terms[rows : 2 * rows]) + terms[2 * rows :]
     answer_copies = []
     for lag in range(DEPTH - 1, -1, -1):
         place = picked.at[0] if lag == 0 else answer.at[lag - 1]
@@ -371,7 +373,6 @@
         sweep, axis = divmod(stage, 2)
         payload, partial = payloads[sweep].at[axis], partials[sweep].at[axis]
         payload[...] = value
-        partial[my_place[axis]] = value
         for other in peers[axis]:
             pltpu.make_async_remote_copy(
                 src_ref=payload,
@@ -381,6 +382,7 @@
                 device_id=other,
                 device_id_type=MESH,
             ).start()
+        partial[my_place[axis]] = value
 
     def others(stage, sems):
         sweep, axis = divmod(stage, 2)

time: 54.6 us -> 54.6 us (level)
  no operation moved by 1% of the time
where the time goes in v5:
time: 54.6 us; the launch traced here: 54.4 us
  Pallas kernels  52.5 us (96%)
  between operations  1.93 us (4%)
    pallas_call x1, Pallas kernels, body(): pl.pallas_call(lambda *refs: kernel(n_tm, n_region, *refs), out_shape=[pl...  51.2 us
    pallas_call x1, Pallas kernels, body(): pl.pallas_call(finish, out_shape=results, in_specs=[vmem] * 4, out_specs=...  1.28 us

profile of v5, /device:TPU:1, one launch (start us, length us, event | category | flops | bytes accessed | tf_op | source)
XLA Modules:
  0.0 54.4 jit_solution(17034281769391762941)
XLA Ops:
  1.9 51.2 %etas_em.1 = (f32[16,16]{1,0:T(8,128)S(1)}, f32[1,1]{1,0:T(1,128)}, f32[24,128]{1,0:T(8,128)S(1)}, f32[24,128]{1,0:T(8,128)S(1)}) custom-call(f32[24,4,128]{2,1,0:T(4,128)} %bitcast.7, f32[24,128]{1,0:T(8,128)} %bitcast.8, f32[16]{0:T(128)} %refs_2_.1, f32[16]{0:T(128)} %refs_3_.1, f32[16,16]{1,0:T(8,128)} %refs_4_.1, f32[1]{0:T(128)S(6)} %copy.13.refs_5_, ...), custom_call_target="tpu_custom_call" | custom-call | tf_op jit(solution)/shard_map/etas_em/pallas_call | solution.py:532
  53.2 1.3 %hand_on.1 = (f32[16,16]{1,0:T(8,128)}, f32[1,1]{1,0:T(1,128)}, f32[24,128]{1,0:T(8,128)}, f32[24,128]{1,0:T(8,128)}) custom-call(f32[16,16]{1,0:T(8,128)S(1)} %get-tuple-element.12.refs_0_, f32[1,1]{1,0:T(1,128)} %get-tuple-element.13.refs_1_, f32[24,128]{1,0:T(8,128)S(1)} %get-tuple-element.14.refs_2_, f32[24,128]{1,0:T(8,128)S(1)} %get-tuple-element.15.refs_3_), custom_call_target="tpu_custom_call" | custom-call | tf_op jit(solution)/shard_map/hand_on/pallas_call | solution.py:591
